TPU v7x, 32 devices: a whole 2x2x4 slice. The times are simulated.
32 devices in a mesh: cfg: 2 (over x), uly: 4 (over y, core), blk: 4 (over z).
Axes of the slice: x: 2, y: 2, z: 4, core: 2. Of those that a mesh axis runs over, the one named last changes fastest.
Arguments:
- queries: bfloat16 [4096, 2048], P(('cfg', 'uly', 'blk')), parts along dimension 0, may hold values from -120 to 120
- keys: bfloat16 [4096, 2048], P(('cfg', 'uly', 'blk')), parts along dimension 0, may hold values from -10 to 10
- values: bfloat16 [4096, 2048], P(('cfg', 'uly', 'blk')), parts along dimension 0, may hold values from -6 to 6
- text_keys: bfloat16 [512, 2048], P('cfg'), parts along dimension 0, may hold values from -9 to 9
- text_values: bfloat16 [512, 2048], P('cfg'), parts along dimension 0, may hold values from -6 to 6
- text_len: int32 [2], P('cfg'), parts along dimension 0, may hold values from 1 to 256
- residual: bfloat16 [4096, 3072], P(('cfg', 'uly', 'blk')), parts along dimension 0, may hold values from -4 to 4
- mlp_term: bfloat16 [4096, 3072], P(('cfg', 'uly', 'blk')), parts along dimension 0, may hold values from -4 to 4
- gate: float32 [3072], replicated, may hold values from 0.5 to 2
- final_shift: float32 [3072], replicated, may hold values from -3 to 3
- final_scale: float32 [3072], replicated, may hold values from -0.5 to 0.5
- final_weight: bfloat16 [3072, 64], replicated, may hold values from -0.109375 to 0.109375
- final_bias: float32 [64], replicated, may hold values from -3 to 3
- out_weight: bfloat16 [2048, 3072], replicated, may hold values from -0.125 to 0.125
- uncond_velocity: float32 [4096, 64], P(('cfg', 'uly', 'blk')), parts along dimension 0, may hold values from -6 to 6
- latents: float32 [4096, 64], P(('cfg', 'uly', 'blk')), parts along dimension 0, may hold values from -6 to 6
- timestep: int32 [1], replicated, may hold values from 0 to 49
- guidance: int32 [1], replicated, may hold values from 15 to 90
Outputs:
- velocity: float32 [4096, 64], P(('cfg', 'uly', 'blk')), parts along dimension 0
- next_latents: float32 [4096, 64], P(('cfg', 'uly', 'blk')), parts along dimension 0
There are 2 independent parts, one for each index of `cfg`. A program takes and returns all parts, laid end to end along the dimension named above; an argument that names none is the same for every part. Nothing has to cross between parts.
All inputs are finite; a program needn't handle non-finite values.
Results may differ from a plain program's by a relative error of at most 0.0065.
Values may be sent and summed in bfloat16 or wider, within the bound.
A program may use at most 128 MiB of HBM per device.

v0:
```python
import math

import jax
import jax.numpy as jnp
from jax import lax
from jax.sharding import PartitionSpec as P

HEADS = 16
HD = 128
STEPS = 50


def power_of_two(exponent):
    shifted = exponent + 64
    result = jnp.full(exponent.shape, 2.0 ** (-64), jnp.float32)
    for position in range(7):
        result = jnp.where(shifted // 2**position % 2 == 1, result * 2.0**2**position, result)
    return result


def floor_log2(magnitude, lowest, highest):
    octave = jnp.full(magnitude.shape, lowest, jnp.int32)
    for degree in range(lowest + 1, highest + 1):
        octave = octave + (magnitude >= 2.0**degree).astype(jnp.int32)
    return octave


def coarse_grid(scaled):
    magnitude = jnp.abs(scaled)
    octave = floor_log2(magnitude, -6, 8)
    ratio = magnitude * power_of_two(3 - octave)
    nearest = jnp.floor(ratio + 0.5)
    halfway = nearest - ratio == 0.5
    is_odd = nearest - 2.0 * jnp.floor(nearest * 0.5) == 1.0
    nearest = jnp.where(halfway & is_odd, nearest - 1.0, nearest)
    return jnp.sign(scaled) * jnp.minimum(nearest * power_of_two(octave - 3), 448.0)


def encode_blocks(entries):
    count, heads_here, width = entries.shape
    blocks = entries.astype(jnp.float32).reshape(count, heads_here, width // 32, 32)
    largest = jnp.max(jnp.abs(blocks), axis=3)
    exponent = floor_log2(largest, -20, 7) - 8
    payload = coarse_grid(blocks * power_of_two(-exponent)[:, :, :, None])
    return (payload.reshape(count, heads_here, width).astype(jnp.bfloat16), exponent)


def decode_blocks(payload, exponent):
    count, heads_here, width = payload.shape
    blocks = payload.astype(jnp.float32).reshape(count, heads_here, width // 32, 32)
    decoded = blocks * power_of_two(exponent)[:, :, :, None]
    return decoded.reshape(count, heads_here, width).astype(jnp.bfloat16)


def text_start(query_rows, text_key_heads, text_value_heads, text_len):
    scaling = 1.0 / math.sqrt(HD)
    scores = (
        jnp.einsum("shd,thd->sht", query_rows, text_key_heads, preferred_element_type=jnp.float32)
        * scaling
    )
    valid = jnp.arange(text_key_heads.shape[0]) < text_len[0]
    scores = jnp.where(valid[None, None, :], scores, -jnp.inf)
    peak = jnp.max(scores, axis=2)
    weights = jnp.exp(scores - peak[:, :, None])
    total = jnp.sum(weights, axis=2)
    summed = jnp.einsum(
        "sht,thd->shd",
        weights.astype(jnp.bfloat16),
        text_value_heads,
        preferred_element_type=jnp.float32,
    )
    return (peak, total, summed)


def attend_block(running, query_rows, block_keys, block_values):
    scaling = 1.0 / math.sqrt(HD)
    peak, total, summed = running
    scores = (
        jnp.einsum("shd,khd->shk", query_rows, block_keys, preferred_element_type=jnp.float32)
        * scaling
    )
    new_peak = jnp.maximum(peak, jnp.max(scores, axis=2))
    correction = jnp.exp(peak - new_peak)
    weights = jnp.exp(scores - new_peak[:, :, None])
    total = total * correction + jnp.sum(weights, axis=2)
    added = jnp.einsum(
        "shk,khd->shd",
        weights.astype(jnp.bfloat16),
        block_values,
        preferred_element_type=jnp.float32,
    )
    summed = summed * correction[:, :, None] + added
    return (new_peak, total, summed)


def key_fold(carried, portion, query_rows):
    key_part, value_part = portion
    count = key_part.shape[0]
    width = 512
    key_blocks = key_part.reshape((count // width, width) + key_part.shape[1:])
    value_blocks = value_part.reshape((count // width, width) + value_part.shape[1:])

    def one_block(running, blocks):
        return (attend_block(running, query_rows, blocks[0], blocks[1]), None)

    final_state, unused = lax.scan(one_block, carried, (key_blocks, value_blocks))
    return final_state


def finish_rows(carried):
    peak, total, summed = carried
    return (summed / total[:, :, None]).astype(jnp.bfloat16)


def sigma_of(moment):
    return 7.0 * moment / (1.0 + 6.0 * moment)


def body(
    queries,
    keys,
    values,
    text_keys,
    text_values,
    text_len,
    residual,
    mlp_term,
    gate,
    final_shift,
    final_scale,
    final_weight,
    final_bias,
    out_weight,
    uncond_velocity,
    latents,
    timestep,
    guidance,
):
    rows_here = queries.shape[0]
    query_three = queries.reshape(rows_here, HEADS, HD)
    key_three = keys.reshape(rows_here, HEADS, HD)
    value_three = values.reshape(rows_here, HEADS, HD)
    text_key_three = text_keys.reshape(text_keys.shape[0], HEADS, HD)
    text_value_three = text_values.reshape(text_values.shape[0], HEADS, HD)
    query_pay, query_exp = encode_blocks(query_three)
    key_pay, key_exp = encode_blocks(key_three)
    value_pay, value_exp = encode_blocks(value_three)
    local_heads = HEADS // lax.axis_size("uly")
    first_head = lax.axis_index("uly") * local_heads
    query_pay, query_exp, key_pay, key_exp, value_pay, value_exp = (
        lax.all_to_all(query_pay, "uly", split_axis=1, concat_axis=0, tiled=True),
        lax.all_to_all(query_exp, "uly", split_axis=1, concat_axis=0, tiled=True),
        lax.all_to_all(key_pay, "uly", split_axis=1, concat_axis=0, tiled=True),
        lax.all_to_all(key_exp, "uly", split_axis=1, concat_axis=0, tiled=True),
        lax.all_to_all(value_pay, "uly", split_axis=1, concat_axis=0, tiled=True),
        lax.all_to_all(value_exp, "uly", split_axis=1, concat_axis=0, tiled=True),
    )
    query_rows = decode_blocks(query_pay, query_exp)
    key_rows = decode_blocks(key_pay, key_exp)
    value_rows = decode_blocks(value_pay, value_exp)
    text_key_heads = lax.dynamic_slice_in_dim(text_key_three, first_head, local_heads, 1)
    text_value_heads = lax.dynamic_slice_in_dim(text_value_three, first_head, local_heads, 1)
    initial = text_start(query_rows, text_key_heads, text_value_heads, text_len)
    carried = key_fold(
        initial,
        (
            lax.all_gather(key_rows, "blk", axis=0, tiled=True),
            lax.all_gather(value_rows, "blk", axis=0, tiled=True),
        ),
        query_rows,
    )
    attention_rows = lax.all_to_all(
        finish_rows(carried), "uly", split_axis=0, concat_axis=1, tiled=True
    )
    attention = attention_rows.reshape(rows_here, HEADS * HD)
    projected = jnp.dot(attention, out_weight, preferred_element_type=jnp.float32)
    hidden = residual.astype(jnp.float32) + gate[None, :] * (
        projected + mlp_term.astype(jnp.float32)
    )
    center = jnp.mean(hidden, axis=1, keepdims=True)
    spread = jnp.mean((hidden - center) ** 2, axis=1, keepdims=True)
    normed = (hidden - center) / jnp.sqrt(spread + 1e-06)
    modulated = (normed * (1.0 + final_scale[None, :]) + final_shift[None, :]).astype(jnp.bfloat16)
    cond_velocity = (
        jnp.dot(modulated, final_weight, preferred_element_type=jnp.float32) + final_bias[None, :]
    )
    factor = guidance[0].astype(jnp.float32) / 10.0
    velocity = uncond_velocity + factor * (cond_velocity - uncond_velocity)
    index = timestep[0].astype(jnp.float32)
    delta = sigma_of(1.0 - (index + 1.0) / STEPS) - sigma_of(1.0 - index / STEPS)
    next_latents = latents + delta * velocity
    return (velocity, next_latents)


def solution(mesh):
    placed = (
        P(("cfg", "uly", "blk"), None),
        P(("cfg", "uly", "blk"), None),
        P(("cfg", "uly", "blk"), None),
        P("cfg", None),
        P("cfg", None),
        P("cfg"),
        P(("cfg", "uly", "blk"), None),
        P(("cfg", "uly", "blk"), None),
        P(),
        P(),
        P(),
        P(),
        P(),
        P(),
        P(("cfg", "uly", "blk"), None),
        P(("cfg", "uly", "blk"), None),
        P(),
        P(),
    )
    return jax.shard_map(
        body,
        mesh=mesh,
        in_specs=placed,
        out_specs=(P(("cfg", "uly", "blk"), None), P(("cfg", "uly", "blk"), None)),
        check_vma=False,
    )
```

profile of v0, /device:TPU:0, one launch (start us, length us, event | category | flops | bytes accessed | tf_op | source)
XLA Modules:
  0.0 184.2 jit_solution(2869041917936696505)
XLA Ops:
  9.7 4.2 %all-to-all-start.3 = ((s32[128,16,4]{0,2,1:T(4,128)}), s32[128,16,4]{0,2,1:T(4,128)S(1)}, u32[]{:S(2)}, u32[]{:S(2)}) async-start(s32[128,16,4]{0,2,1:T(4,128)} %copy.167), calls=%async_computation.3 | async-start | bytes 65536 | tf_op jit(solution)/shard_map/all_to_all | solution.py:154
  13.9 14.9 %fusion.92 = bf16[128,16,128]{0,2,1:T(8,128)(2,1)} fusion(f32[128,16,4]{0,2,1:T(4,128)S(1)} %copy.165, bf16[128,16,128]{0,2,1:T(8,128)(2,1)S(1)} %bitcast.138), kind=kLoop, calls=%fused_computation.366 | loop fusion | flops 98304000 | bytes 1081344 | tf_op jit(solution)/shard_map/convert_element_type | solution.py:45
  28.9 3.5 %all-to-all-start.2 = ((bf16[128,16,128]{0,2,1:T(8,128)(2,1)}), bf16[128,16,128]{0,2,1:T(8,128)(2,1)S(1)}, u32[]{:S(2)}, u32[]{:S(2)}) async-start(bf16[128,16,128]{0,2,1:T(8,128)(2,1)} %fusion.92), calls=%async_computation.2 | async-start | bytes 1048576 | tf_op jit(solution)/shard_map/all_to_all | solution.py:153
  33.3 7.9 %all-to-all-done.2 = bf16[128,16,128]{0,2,1:T(8,128)(2,1)S(1)} async-done(((bf16[128,16,128]{0,2,1:T(8,128)(2,1)}), bf16[128,16,128]{0,2,1:T(8,128)(2,1)S(1)}, u32[]{:S(2)}, u32[]{:S(2)}) %all-to-all-start.2) | async-done | bytes 524320 | tf_op jit(solution)/shard_map/all_to_all | solution.py:153
  43.7 3.3 %all-to-all-start.5 = ((s32[128,16,4]{0,2,1:T(4,128)}), s32[128,16,4]{0,2,1:T(4,128)S(1)}, u32[]{:S(2)}, u32[]{:S(2)}) async-start(s32[128,16,4]{0,2,1:T(4,128)} %copy.201), calls=%async_computation.5 | async-start | bytes 65536 | tf_op jit(solution)/shard_map/all_to_all | solution.py:156
  47.0 14.9 %fusion.133 = bf16[128,16,128]{0,2,1:T(8,128)(2,1)} fusion(f32[128,16,4]{0,2,1:T(4,128)S(1)} %copy.199, bf16[128,16,128]{0,2,1:T(8,128)(2,1)S(1)} %bitcast.139), kind=kLoop, calls=%fused_computation.407 | loop fusion | flops 98304000 | bytes 1081344 | tf_op jit(solution)/shard_map/convert_element_type | solution.py:45
  61.9 3.5 %all-to-all-start.4 = ((bf16[128,16,128]{0,2,1:T(8,128)(2,1)}), bf16[128,16,128]{0,2,1:T(8,128)(2,1)S(1)}, u32[]{:S(2)}, u32[]{:S(2)}) async-start(bf16[128,16,128]{0,2,1:T(8,128)(2,1)} %fusion.133), calls=%async_computation.4 | async-start | bytes 1048576 | tf_op jit(solution)/shard_map/all_to_all | solution.py:155
  66.4 7.9 %all-to-all-done.4 = bf16[128,16,128]{0,2,1:T(8,128)(2,1)S(1)} async-done(((bf16[128,16,128]{0,2,1:T(8,128)(2,1)}), bf16[128,16,128]{0,2,1:T(8,128)(2,1)S(1)}, u32[]{:S(2)}, u32[]{:S(2)}) %all-to-all-start.4) | async-done | bytes 524320 | tf_op jit(solution)/shard_map/all_to_all | solution.py:155
  78.0 3.3 %all-to-all-start.1 = ((s32[128,16,4]{0,2,1:T(4,128)}), s32[128,16,4]{0,2,1:T(4,128)S(1)}, u32[]{:S(2)}, u32[]{:S(2)}) async-start(s32[128,16,4]{0,2,1:T(4,128)} %copy.131), calls=%async_computation.1 | async-start | bytes 65536 | tf_op jit(solution)/shard_map/all_to_all | solution.py:152
  84.6 14.9 %fusion.51 = bf16[128,16,128]{0,2,1:T(8,128)(2,1)} fusion(f32[128,16,4]{0,2,1:T(4,128)S(1)} %copy.128, bf16[128,16,128]{0,2,1:T(8,128)(2,1)S(1)} %bitcast.137), kind=kLoop, calls=%fused_computation.325 | loop fusion | flops 98304000 | bytes 1081344 | tf_op jit(solution)/shard_map/convert_element_type | solution.py:45
  99.5 3.7 %all-to-all-start = ((bf16[128,16,128]{0,2,1:T(8,128)(2,1)}), bf16[128,16,128]{0,2,1:T(8,128)(2,1)S(1)}, u32[]{:S(2)}, u32[]{:S(2)}) async-start(bf16[128,16,128]{0,2,1:T(8,128)(2,1)} %fusion.51), calls=%async_computation | async-start | bytes 1048576 | tf_op jit(solution)/shard_map/all_to_all | solution.py:151
  104.0 7.9 %all-to-all-done = bf16[128,16,128]{0,2,1:T(8,128)(2,1)S(1)} async-done(((bf16[128,16,128]{0,2,1:T(8,128)(2,1)}), bf16[128,16,128]{0,2,1:T(8,128)(2,1)S(1)}, u32[]{:S(2)}, u32[]{:S(2)}) %all-to-all-start) | async-done | bytes 524320 | tf_op jit(solution)/shard_map/all_to_all | solution.py:151
  118.4 17.3 %all-gather.5.cloned.1.call-done = bf16[2048,4,128]{2,0,1:T(8,128)(2,1)} async-done(((bf16[512,4,128]{2,0,1:T(8,128)(2,1)}), bf16[2048,4,128]{2,0,1:T(8,128)(2,1)}) %all-gather.5.cloned.1.call-update) | async-done | bytes 2097168 | tf_op jit(solution)/shard_map/all_gather | solution.py:168
  135.7 18.5 %while.14 = (s32[]{:T(128)}, f32[512,4]{0,1:T(4,128)S(1)}, f32[512,4]{0,1:T(4,128)S(1)}, f32[512,4,128]{0,2,1:T(8,128)S(1)}, bf16[4,512,4,128]{3,1,0,2:T(8,128)(...) while((s32[]{:T(128)}, f32[512,4]{0,1:T(4,128)S(1)}, ...), condition=%wide.region_8.9_spmd, body=%wide.region_5.8_spmd.sunk | while | flops 545787904 | bytes 16385109 | solution.py:106
  138.2 2.1 %fusion.338 = f32[512,4,128]{0,2,1:T(8,128)S(1)} fusion(f32[4,512,512]{2,1,0:T(8,128)S(1)} %get-tuple-element.148, f32[512,4]{0,1:T(4,128)S(1)} %max.4, f32[512,4,128]{0,2,1:T(8,128)S(1)} %get-tuple-element.162, bf16[4,512,4,128]{3,1,0,2:T(8,128)(2,1)} %get-tuple-element.173, s32[]{:T(128)} %get-tuple-element.159, f32[512,4]{0,1:T(4,128)S(1)} %get-tuple-element.150), kind=kOutput, calls=%fused_computation.9.clone.1 | convolution fusion | flops 272105472 | bytes 6832640 | tf_op jit(solution)/shard_map/while/body/eval_jaxpr/shk,khd->shd/dot_general | solution.py:86
  140.4 1.8 bitcast_reduce_fusion.6
  142.9 2.1 %fusion.338 = f32[512,4,128]{0,2,1:T(8,128)S(1)} fusion(f32[4,512,512]{2,1,0:T(8,128)S(1)} %get-tuple-element.148, f32[512,4]{0,1:T(4,128)S(1)} %max.4, f32[512,4,128]{0,2,1:T(8,128)S(1)} %get-tuple-element.162, bf16[4,512,4,128]{3,1,0,2:T(8,128)(2,1)} %get-tuple-element.173, s32[]{:T(128)} %get-tuple-element.159, f32[512,4]{0,1:T(4,128)S(1)} %get-tuple-element.150), kind=kOutput, calls=%fused_computation.9.clone.1 | convolution fusion | flops 272105472 | bytes 6832640 | tf_op jit(solution)/shard_map/while/body/eval_jaxpr/shk,khd->shd/dot_general | solution.py:86
  145.0 1.8 bitcast_reduce_fusion.6
  147.5 2.1 %fusion.338 = f32[512,4,128]{0,2,1:T(8,128)S(1)} fusion(f32[4,512,512]{2,1,0:T(8,128)S(1)} %get-tuple-element.148, f32[512,4]{0,1:T(4,128)S(1)} %max.4, f32[512,4,128]{0,2,1:T(8,128)S(1)} %get-tuple-element.162, bf16[4,512,4,128]{3,1,0,2:T(8,128)(2,1)} %get-tuple-element.173, s32[]{:T(128)} %get-tuple-element.159, f32[512,4]{0,1:T(4,128)S(1)} %get-tuple-element.150), kind=kOutput, calls=%fused_computation.9.clone.1 | convolution fusion | flops 272105472 | bytes 6832640 | tf_op jit(solution)/shard_map/while/body/eval_jaxpr/shk,khd->shd/dot_general | solution.py:86
  149.6 1.8 bitcast_reduce_fusion.6
  152.2 2.1 %fusion.338 = f32[512,4,128]{0,2,1:T(8,128)S(1)} fusion(f32[4,512,512]{2,1,0:T(8,128)S(1)} %get-tuple-element.148, f32[512,4]{0,1:T(4,128)S(1)} %max.4, f32[512,4,128]{0,2,1:T(8,128)S(1)} %get-tuple-element.162, bf16[4,512,4,128]{3,1,0,2:T(8,128)(2,1)} %get-tuple-element.173, s32[]{:T(128)} %get-tuple-element.159, f32[512,4]{0,1:T(4,128)S(1)} %get-tuple-element.150), kind=kOutput, calls=%fused_computation.9.clone.1 | convolution fusion | flops 272105472 | bytes 6832640 | tf_op jit(solution)/shard_map/while/body/eval_jaxpr/shk,khd->shd/dot_general | solution.py:86
  156.3 3.6 %all-to-all-start.6 = ((bf16[512,4,128]{2,1,0:T(4,128)(2,1)}), bf16[512,4,128]{2,1,0:T(4,128)(2,1)S(1)}, u32[]{:S(2)}, u32[]{:S(2)}) async-start(bf16[512,4,128]{2,1,0:T(4,128)(2,1)} %divide_convert_fusion), calls=%async_computation.6 | async-start | bytes 1048576 | tf_op jit(solution)/shard_map/all_to_all | solution.py:172
  161.3 7.4 %all-to-all-done.6 = bf16[512,4,128]{2,1,0:T(4,128)(2,1)S(1)} async-done(((bf16[512,4,128]{2,1,0:T(4,128)(2,1)}), bf16[512,4,128]{2,1,0:T(4,128)(2,1)S(1)}, u32[]{:S(2)}, u32[]{:S(2)}) %all-to-all-start.6) | async-done | bytes 524320 | tf_op jit(solution)/shard_map/all_to_all | solution.py:172
  169.1 6.7 %fusion.323 = (f32[128]{0:T(128)S(1)}, f32[128,3072]{1,0:T(8,128)S(1)}) fusion(bf16[128,3072]{1,0:T(8,128)(2,1)S(1)} %copy-done.3, bf16[128,2048]{0,1:T(8,128)(2,1)S(1)} %bitcast.146, bf16[2048,3072]{1,0:T(8,128)(2,1)} %param.33, f32[3072]{0:T(1024)S(1)} %copy-done.6, bf16[128,3072]{1,0:T(8,128)(2,1)S(1)} %copy-done.4), kind=kOutput, calls=%fused_computation.911 | convolution fusion | flops 1612971904 | bytes 16265728 | tf_op jit(solution)/shard_map/dot_general | solution.py:176
  (105 shorter events, 29.0 us)
Async XLA Ops:
  7.2 169.1 %copy-start = (bf16[3072,64]{0,1:T(8,128)(2,1)S(1)}, bf16[3072,64]{0,1:T(8,128)(2,1)}, u32[]{:S(2)}) copy-start(bf16[3072,64]{0,1:T(8,128)(2,1)} %param.31) | copy-start | bytes 1179652
  9.7 19.2 %all-to-all-start.3 = ((s32[128,16,4]{0,2,1:T(4,128)}), s32[128,16,4]{0,2,1:T(4,128)S(1)}, u32[]{:S(2)}, u32[]{:S(2)}) async-start(s32[128,16,4]{0,2,1:T(4,128)} %copy.167), calls=%async_computation.3 | async-start | bytes 65536 | tf_op jit(solution)/shard_map/all_to_all | solution.py:154
  28.9 12.3 %all-to-all-start.2 = ((bf16[128,16,128]{0,2,1:T(8,128)(2,1)}), bf16[128,16,128]{0,2,1:T(8,128)(2,1)S(1)}, u32[]{:S(2)}, u32[]{:S(2)}) async-start(bf16[128,16,128]{0,2,1:T(8,128)(2,1)} %fusion.92), calls=%async_computation.2 | async-start | bytes 1048576 | tf_op jit(solution)/shard_map/all_to_all | solution.py:153
  32.3 86.1 %all-gather.3.cloned.1.call-start = ((), (), s32[]{:S(2)}) async-start(), calls=%async_computation.7 | async-start | bytes 2621440 | tf_op jit(solution)/shard_map/all_gather | solution.py:167
  41.1 1.2 copy-start.5
  43.7 18.2 %all-to-all-start.5 = ((s32[128,16,4]{0,2,1:T(4,128)}), s32[128,16,4]{0,2,1:T(4,128)S(1)}, u32[]{:S(2)}, u32[]{:S(2)}) async-start(s32[128,16,4]{0,2,1:T(4,128)} %copy.201), calls=%async_computation.5 | async-start | bytes 65536 | tf_op jit(solution)/shard_map/all_to_all | solution.py:156
  61.9 12.3 %all-to-all-start.4 = ((bf16[128,16,128]{0,2,1:T(8,128)(2,1)}), bf16[128,16,128]{0,2,1:T(8,128)(2,1)S(1)}, u32[]{:S(2)}, u32[]{:S(2)}) async-start(bf16[128,16,128]{0,2,1:T(8,128)(2,1)} %fusion.133), calls=%async_computation.4 | async-start | bytes 1048576 | tf_op jit(solution)/shard_map/all_to_all | solution.py:155
  65.4 70.3 %all-gather.5.cloned.1.call-start = ((), (), s32[]{:S(2)}) async-start(), calls=%async_computation.8 | async-start | bytes 2621440 | tf_op jit(solution)/shard_map/all_gather | solution.py:168
  74.4 7.5 %copy-start.1 = (bf16[256,2048]{1,0:T(8,128)(2,1)S(1)}, bf16[256,2048]{1,0:T(8,128)(2,1)}, u32[]{:S(2)}) copy-start(bf16[256,2048]{1,0:T(8,128)(2,1)} %param.23) | copy-start | bytes 3145732
  75.4 7.8 %copy-start.2 = (bf16[256,2048]{1,0:T(8,128)(2,1)S(1)}, bf16[256,2048]{1,0:T(8,128)(2,1)}, u32[]{:S(2)}) copy-start(bf16[256,2048]{1,0:T(8,128)(2,1)} %param.24) | copy-start | bytes 3145732
  78.0 21.5 %all-to-all-start.1 = ((s32[128,16,4]{0,2,1:T(4,128)}), s32[128,16,4]{0,2,1:T(4,128)S(1)}, u32[]{:S(2)}, u32[]{:S(2)}) async-start(s32[128,16,4]{0,2,1:T(4,128)} %copy.131), calls=%async_computation.1 | async-start | bytes 65536 | tf_op jit(solution)/shard_map/all_to_all | solution.py:152
  99.5 12.4 %all-to-all-start = ((bf16[128,16,128]{0,2,1:T(8,128)(2,1)}), bf16[128,16,128]{0,2,1:T(8,128)(2,1)S(1)}, u32[]{:S(2)}, u32[]{:S(2)}) async-start(bf16[128,16,128]{0,2,1:T(8,128)(2,1)} %fusion.51), calls=%async_computation | async-start | bytes 1048576 | tf_op jit(solution)/shard_map/all_to_all | solution.py:151
  154.7 6.6 %copy-start.7 = (f32[3072]{0:T(1024)S(1)}, f32[3072]{0:T(1024)}, u32[]{:S(2)}) copy-start(f32[3072]{0:T(1024)} %param.30) | copy-start | bytes 36868
  154.8 14.2 %copy-start.6 = (f32[3072]{0:T(1024)S(1)}, f32[3072]{0:T(1024)}, u32[]{:S(2)}) copy-start(f32[3072]{0:T(1024)} %param.28) | copy-start | bytes 36868
  156.3 12.8 %copy-start.3 = (bf16[128,3072]{1,0:T(8,128)(2,1)S(1)}, bf16[128,3072]{1,0:T(8,128)(2,1)}, u32[]{:S(2)}) copy-start(bf16[128,3072]{1,0:T(8,128)(2,1)} %param.27) | copy-start | bytes 2359300
  156.3 12.8 %copy-start.4 = (bf16[128,3072]{1,0:T(8,128)(2,1)S(1)}, bf16[128,3072]{1,0:T(8,128)(2,1)}, u32[]{:S(2)}) copy-start(bf16[128,3072]{1,0:T(8,128)(2,1)} %param.26) | copy-start | bytes 2359300
  156.3 12.4 %all-to-all-start.6 = ((bf16[512,4,128]{2,1,0:T(4,128)(2,1)}), bf16[512,4,128]{2,1,0:T(4,128)(2,1)S(1)}, u32[]{:S(2)}, u32[]{:S(2)}) async-start(bf16[512,4,128]{2,1,0:T(4,128)(2,1)} %divide_convert_fusion), calls=%async_computation.6 | async-start | bytes 1048576 | tf_op jit(solution)/shard_map/all_to_all | solution.py:172
  169.1 7.1 %copy-start.8 = (f32[128,64]{0,1:T(8,128)S(1)}, f32[128,64]{0,1:T(8,128)}, u32[]{:S(2)}) copy-start(f32[128,64]{0,1:T(8,128)} %param.35) | copy-start | bytes 98308
  169.1 7.1 %copy-start.9 = (f32[128,64]{0,1:T(8,128)S(1)}, f32[128,64]{0,1:T(8,128)}, u32[]{:S(2)}) copy-start(f32[128,64]{0,1:T(8,128)} %param.34) | copy-start | bytes 98308
  169.1 7.1 %copy-start.10 = (f32[3072]{0:T(1024)S(1)}, f32[3072]{0:T(1024)}, u32[]{:S(2)}) copy-start(f32[3072]{0:T(1024)} %param.29) | copy-start | bytes 36868
  169.1 7.1 %copy-start.11 = (f32[64]{0:T(128)S(1)}, f32[64]{0:T(128)}, u32[]{:S(2)}) copy-start(f32[64]{0:T(128)} %param.32) | copy-start | bytes 772
Sparse Core Ops, SparseCore 0:
  42.4 46.9 all-gather.2
  90.9 44.7 all-gather.4
where the time goes:
time: 185 us; the launch traced here: 184 us
  other arithmetic  55.6 us (30%)
  waiting for transfers between devices  48.4 us (26%)
  matrix products  26.5 us (14%)
  starting transfers between devices  25 us (14%)
  between operations  16.6 us (9%)
  local copies, waits for them, and re-layouts  12 us (6%)
    convert_element_type x3, other arithmetic, encode_blocks(): payload.reshape(count, heads_here, width).astype(jnp.bfloat16)  44.8 us
    all_gather x1, waiting for transfers between devices, body(): lax.all_gather(value_rows, 'blk', axis=0, tiled=True)  17.3 us
    dot_general x4, matrix products, attend_block(): jnp.einsum('shk,khd->shd', weights.astype(jnp.bfloat16), block_values, pr...  8.37 us
    all_to_all x1, waiting for transfers between devices, body(): lax.all_to_all(query_pay, 'uly', split_axis=1, concat_axis=0, tiled=True)  7.89 us
    all_to_all x1, waiting for transfers between devices, body(): lax.all_to_all(key_pay, 'uly', split_axis=1, concat_axis=0, tiled=True)  7.87 us
    all_to_all x1, waiting for transfers between devices, body(): lax.all_to_all(value_pay, 'uly', split_axis=1, concat_axis=0, tiled=True)  7.86 us
    all_to_all x1, waiting for transfers between devices, body(): lax.all_to_all(finish_rows(carried), 'uly', split_axis=0, concat_axis=1,...  7.4 us
    dot_general x4, matrix products, attend_block(): jnp.einsum('shd,khd->shk', query_rows, block_keys, preferred_element_type...  7.07 us
  transfers between devices with their start and end apart: 9, of which 5 were waited for; matrix products, arithmetic and copies ran while one was open for 33% of the time, Pallas kernels for 0%

commit v1 on v0

--- a/solution.py
+++ b/solution.py
@@ -1,8 +1,11 @@
+import functools
 import math
 
 import jax
 import jax.numpy as jnp
 from jax import lax
+from jax.experimental import pallas as pl
+from jax.experimental.pallas import tpu as pltpu
 from jax.sharding import PartitionSpec as P
 
 HEADS = 16
@@ -192,6 +195,373 @@
     return (velocity, next_latents)
 
 
+CHUNK = 2
+
+
+def block_round(entries, spread_matrix):
+    x = entries.astype(jnp.float32)
+    size = jnp.abs(x)
+    top = size
+    for shift in (1, 2, 4, 8, 16):
+        top = jnp.maximum(top, pltpu.roll(top, shift, 1))
+    top = jnp.maximum(top, 2.0**-20)
+    top = top * 0.7515
+    carrier = top * 2.0**23
+    top = (top + carrier) - carrier
+    scale = jnp.dot(
+        top.astype(jnp.bfloat16), spread_matrix, preferred_element_type=jnp.float32
+    )
+    carrier = jnp.maximum(size * 2.0**20, scale * 96.0)
+    rounded = (x + carrier) - carrier
+    limit = scale * 1.75
+    return jnp.minimum(jnp.maximum(rounded, -limit), limit).astype(jnp.bfloat16)
+
+
+def fused_kernel(
+    uly_size,
+    blk_size,
+    q_hbm,
+    k_hbm,
+    v_hbm,
+    tk_hbm,
+    tv_hbm,
+    text_len,
+    res_hbm,
+    mlp_hbm,
+    gate,
+    shift,
+    scale,
+    fw_hbm,
+    bias,
+    ow_hbm,
+    uncond,
+    latents,
+    timestep,
+    guidance,
+    vel_out,
+    next_out,
+    raw,
+    coded,
+    qbuf,
+    kbuf,
+    vbuf,
+    obuf,
+    att,
+    weight,
+    res,
+    mlp,
+    fw,
+    load_sem,
+    weight_sem,
+    send_sem,
+    recv_sem,
+    osend_sem,
+    orecv_sem,
+):
+    n = uly_size * blk_size
+    rows = raw.shape[1]
+    uly = lax.axis_index("uly")
+    blk = lax.axis_index("blk")
+    me = uly * blk_size + blk
+
+    def ahead(j):
+        return lax.rem(uly + lax.rem(j, uly_size), uly_size), lax.rem(
+            blk + j // uly_size, blk_size
+        )
+
+    def behind(j):
+        return lax.rem(uly + uly_size - lax.rem(j, uly_size), uly_size), lax.rem(
+            blk + blk_size - j // uly_size, blk_size
+        )
+
+    barrier = pltpu.get_barrier_semaphore()
+
+    def greet(j, unused):
+        u, b = ahead(j)
+        pl.semaphore_signal(
+            barrier, inc=1, device_id={"uly": u, "blk": b}, device_id_type=pl.DeviceIdType.MESH
+        )
+        return unused
+
+    own = pl.ds(pl.multiple_of(me * HD, HD), HD)
+    text = tk_hbm.shape[0]
+    loads = [
+        pltpu.make_async_copy(k_hbm, raw.at[0], load_sem.at[0]),
+        pltpu.make_async_copy(v_hbm, raw.at[1], load_sem.at[1]),
+        pltpu.make_async_copy(q_hbm, raw.at[2], load_sem.at[2]),
+        pltpu.make_async_copy(tk_hbm.at[:, own], kbuf.at[pl.ds(n * rows, text)], load_sem.at[3]),
+        pltpu.make_async_copy(tv_hbm.at[:, own], vbuf.at[pl.ds(n * rows, text)], load_sem.at[4]),
+        pltpu.make_async_copy(res_hbm, res, load_sem.at[5]),
+        pltpu.make_async_copy(mlp_hbm, mlp, load_sem.at[6]),
+        pltpu.make_async_copy(fw_hbm, fw, load_sem.at[7]),
+    ]
+    for load in loads:
+        load.start()
+    lax.fori_loop(1, n, greet, 0)
+
+    lane_from = lax.broadcasted_iota(jnp.int32, (HD, HD), 0)
+    lane_to = lax.broadcasted_iota(jnp.int32, (HD, HD), 1)
+    spread_matrix = jnp.where(lane_from == lane_to // 32 * 32 + 31, 1.0, 0.0).astype(jnp.bfloat16)
+
+    def slot(j):
+        return pl.ds(pl.multiple_of(j * rows, rows), rows)
+
+    def outgoing(kind, target, j):
+        u, b = ahead(j)
+        return pltpu.make_async_remote_copy(
+            src_ref=coded.at[kind, slot(j)],
+            dst_ref=target.at[slot(j)],
+            send_sem=send_sem.at[kind, j],
+            recv_sem=recv_sem.at[kind, j],
+            device_id={"uly": u, "blk": b},
+            device_id_type=pl.DeviceIdType.MESH,
+        )
+
+    def weight_load(j):
+        u, b = ahead(j)
+        start = pl.multiple_of((u * blk_size + b) * HD, HD)
+        return pltpu.make_async_copy(
+            ow_hbm.at[pl.ds(start, HD)], weight.at[slot(j) if rows == HD else pl.ds(j * HD, HD)],
+            weight_sem.at[j],
+        )
+
+    for kind, target in ((0, kbuf), (1, vbuf), (2, qbuf)):
+        loads[kind].wait()
+
+        def code(j):
+            u, b = ahead(j)
+            columns = pl.ds(pl.multiple_of((u * blk_size + b) * HD, HD), HD)
+            return block_round(raw[kind, :, columns], spread_matrix)
+
+        if kind == 0:
+
+            def code_only(i, unused):
+                j = n - 1 - i
+                coded[kind, slot(j), :] = code(j)
+                return unused
+
+            lax.fori_loop(0, 2, code_only, 0)
+            pl.semaphore_wait(barrier, n - 1)
+            outgoing(kind, target, n - 1).start()
+            outgoing(kind, target, n - 2).start()
+            first = 2
+        else:
+            first = 0
+
+        def code_and_send(i, unused):
+            j = n - 1 - i
+            coded[kind, slot(j), :] = code(j)
+            outgoing(kind, target, j).start()
+            return unused
+
+        lax.fori_loop(first, n - 1, code_and_send, 0)
+        target[pl.ds(0, rows), :] = code(0)
+
+    def start_weight(i, unused):
+        weight_load(n - 1 - i).start()
+        return unused
+
+    lax.fori_loop(0, n, start_weight, 0)
+
+    def wait_recv(kind, target):
+        def one(i, unused):
+            outgoing(kind, target, n - 1 - i).wait_recv()
+            return unused
+
+        lax.fori_loop(0, n - 1, one, 0)
+
+    wait_recv(0, kbuf)
+    wait_recv(1, vbuf)
+    loads[3].wait()
+    loads[4].wait()
+
+    factor = math.log2(math.e) / math.sqrt(HD)
+    span = CHUNK * rows
+    text_valid = lax.broadcasted_iota(jnp.int32, (span, text), 1) < text_len[0]
+
+    def attend(first_slot):
+        q = qbuf[pl.ds(pl.multiple_of(first_slot * rows, rows), span), :]
+        across = (((1,), (1,)), ((), ()))
+        image = lax.dot_general(
+            q, kbuf[pl.ds(0, n * rows), :], across, preferred_element_type=jnp.float32
+        )
+        words = lax.dot_general(
+            q, kbuf[pl.ds(n * rows, text), :], across, preferred_element_type=jnp.float32
+        )
+        words = jnp.where(text_valid, words, -jnp.inf)
+        peak = jnp.maximum(
+            jnp.max(image, axis=1, keepdims=True), jnp.max(words, axis=1, keepdims=True)
+        )
+        image = jnp.exp2((image - peak) * factor)
+        words = jnp.exp2((words - peak) * factor)
+        total = jnp.sum(image, axis=1, keepdims=True) + jnp.sum(words, axis=1, keepdims=True)
+        mixed = jnp.dot(
+            image.astype(jnp.bfloat16),
+            vbuf[pl.ds(0, n * rows), :],
+            preferred_element_type=jnp.float32,
+        ) + jnp.dot(
+            words.astype(jnp.bfloat16),
+            vbuf[pl.ds(n * rows, text), :],
+            preferred_element_type=jnp.float32,
+        )
+        return (mixed / total).astype(jnp.bfloat16)
+
+    def returning(j):
+        u, b = behind(j)
+        return pltpu.make_async_remote_copy(
+            src_ref=obuf.at[slot(j)],
+            dst_ref=att.at[j],
+            send_sem=osend_sem.at[j],
+            recv_sem=orecv_sem.at[j],
+            device_id={"uly": u, "blk": b},
+            device_id_type=pl.DeviceIdType.MESH,
+        )
+
+    def chunk(c, unused):
+        first_slot = n - CHUNK - c * CHUNK
+        for k in range(CHUNK):
+            outgoing(2, qbuf, first_slot + k).wait_recv()
+        obuf[pl.ds(pl.multiple_of(first_slot * rows, rows), span), :] = attend(first_slot)
+        for k in range(CHUNK):
+            returning(first_slot + k).start()
+        return unused
+
+    lax.fori_loop(0, n // CHUNK - 1, chunk, 0)
+    for k in range(1, CHUNK):
+        outgoing(2, qbuf, k).wait_recv()
+    mixed = attend(0)
+    obuf[pl.ds(0, span), :] = mixed
+    for k in range(1, CHUNK):
+        returning(k).start()
+    att[0] = mixed[:rows]
+
+    hidden = jnp.zeros((rows, gate.shape[1]), jnp.float32)
+    group = 4
+    for g in range(n // group - 1, -1, -1):
+        for j in range(g * group, (g + 1) * group):
+            weight_load(j).wait()
+            if j > 0:
+                returning(j).wait_recv()
+        here = jnp.concatenate([att[j] for j in range(g * group, (g + 1) * group)], axis=1)
+        hidden = hidden + jnp.dot(
+            here,
+            weight[pl.ds(g * group * HD, group * HD), :],
+            preferred_element_type=jnp.float32,
+        )
+    loads[5].wait()
+    loads[6].wait()
+    hidden = res[...].astype(jnp.float32) + gate[...] * (hidden + mlp[...].astype(jnp.float32))
+    center = jnp.mean(hidden, axis=1, keepdims=True)
+    hidden = hidden - center
+    variance = jnp.mean(hidden * hidden, axis=1, keepdims=True)
+    hidden = hidden * (1.0 / jnp.sqrt(variance + 1e-06))
+    modulated = (hidden * (1.0 + scale[...]) + shift[...]).astype(jnp.bfloat16)
+    loads[7].wait()
+    cond = lax.dot_general(
+        fw[...], modulated, (((1,), (1,)), ((), ())), preferred_element_type=jnp.float32
+    ) + jnp.transpose(jnp.broadcast_to(bias[...], (rows, bias.shape[1])))
+    strength = jnp.full((1, 1), guidance[0], jnp.int32).astype(jnp.float32) / 10.0
+    velocity = uncond[...] + strength * (cond - uncond[...])
+    index = jnp.full((1, 1), timestep[0], jnp.int32).astype(jnp.float32)
+    delta = sigma_of(1.0 - (index + 1.0) / STEPS) - sigma_of(1.0 - index / STEPS)
+    vel_out[...] = velocity
+    next_out[...] = latents[...] + delta * velocity
+
+    def drain(j, unused):
+        outgoing(0, kbuf, j).wait_send()
+        outgoing(1, vbuf, j).wait_send()
+        outgoing(2, qbuf, j).wait_send()
+        returning(j).wait_send()
+        return unused
+
+    lax.fori_loop(1, n, drain, 0)
+
+
+def fused_body(
+    queries,
+    keys,
+    values,
+    text_keys,
+    text_values,
+    text_len,
+    residual,
+    mlp_term,
+    gate,
+    final_shift,
+    final_scale,
+    final_weight,
+    final_bias,
+    out_weight,
+    uncond_velocity,
+    latents,
+    timestep,
+    guidance,
+):
+    uly_size = lax.axis_size("uly")
+    blk_size = lax.axis_size("blk")
+    n = uly_size * blk_size
+    rows = queries.shape[0]
+    text = text_keys.shape[0]
+    width = residual.shape[1]
+    anywhere = pl.BlockSpec(memory_space=pl.ANY)
+    vmem = pl.BlockSpec(memory_space=pltpu.VMEM)
+    smem = pl.BlockSpec(memory_space=pltpu.SMEM)
+    result = jax.ShapeDtypeStruct(latents.shape[::-1], jnp.float32)
+    bf16 = jnp.bfloat16
+    velocity, next_latents = pl.pallas_call(
+        functools.partial(fused_kernel, uly_size, blk_size),
+        out_shape=(result, result),
+        in_specs=[anywhere] * 5
+        + [smem]
+        + [anywhere] * 2
+        + [vmem] * 3
+        + [anywhere, vmem, anywhere, vmem, vmem, smem, smem],
+        out_specs=(vmem, vmem),
+        scratch_shapes=[
+            pltpu.VMEM((3, rows, HEADS * HD), bf16),
+            pltpu.VMEM((3, n * rows, HD), bf16),
+            pltpu.VMEM((n * rows, HD), bf16),
+            pltpu.VMEM((n * rows + text, HD), bf16),
+            pltpu.VMEM((n * rows + text, HD), bf16),
+            pltpu.VMEM((n * rows, HD), bf16),
+            pltpu.VMEM((n, rows, HD), bf16),
+            pltpu.VMEM((HEADS * HD, width), bf16),
+            pltpu.VMEM((rows, width), bf16),
+            pltpu.VMEM((rows, width), bf16),
+            pltpu.VMEM(final_weight.shape[::-1], bf16),
+            pltpu.SemaphoreType.DMA((8,)),
+            pltpu.SemaphoreType.DMA((n,)),
+            pltpu.SemaphoreType.DMA((3, n)),
+            pltpu.SemaphoreType.DMA((3, n)),
+            pltpu.SemaphoreType.DMA((n,)),
+            pltpu.SemaphoreType.DMA((n,)),
+        ],
+        compiler_params=pltpu.CompilerParams(
+            collective_id=0, has_side_effects=True, vmem_limit_bytes=56 * 2**20
+        ),
+    )(
+        queries,
+        keys,
+        values,
+        text_keys,
+        text_values,
+        text_len,
+        residual,
+        mlp_term,
+        gate.reshape(1, width),
+        final_shift.reshape(1, width),
+        final_scale.reshape(1, width),
+        final_weight.T,
+        final_bias.reshape(1, -1),
+        out_weight,
+        uncond_velocity.T,
+        latents.T,
+        timestep,
+        guidance,
+    )
+    return velocity.T, next_latents.T
+
+
 def solution(mesh):
     placed = (
         P(("cfg", "uly", "blk"), None),
@@ -214,7 +584,7 @@
         P(),
     )
     return jax.shard_map(
-        body,
+        fused_body if mesh.shape["uly"] * mesh.shape["blk"] == HEADS else body,
         mesh=mesh,
         in_specs=placed,
         out_specs=(P(("cfg", "uly", "blk"), None), P(("cfg", "uly", "blk"), None)),

time: 185 us -> 67.1 us (0.36)
  Pallas kernels: 0 us -> 60.7 us
  other arithmetic: 55.6 us -> 0 us
  waiting for transfers between devices: 48.4 us -> 0 us
  matrix products: 26.5 us -> 0 us
  starting transfers between devices: 25 us -> 0 us
  between operations: 16.6 us -> 2.58 us
  local copies, waits for them, and re-layouts: 12 us -> 2.75 us
    pallas_call x0 -> x1, Pallas kernels: none -> 60.7 us  [fused_body(): pl.pallas_call(functools.partial(fused_kernel, uly_size, blk_size), out_s...]
    convert_element_type x8 -> x0, other arithmetic: 49.2 us -> none  [the longest x3 44.8 us: encode_blocks(): payload.reshape(count, heads_here, width).astype(jnp.bfloat16)]
    all_to_all x7 -> x0, waiting for transfers between devices: 31 us -> none  [the longest x1 7.89 us: body(): lax.all_to_all(query_pay, 'uly', split_axis=1, concat_axis=0, tiled=True)]
    dot_general x12 -> x0, matrix products: 26.5 us -> none  [the longest x4 8.37 us: attend_block(): jnp.einsum('shk,khd->shd', weights.astype(jnp.bfloat16), block_values, pr...]
    all_to_all x7 -> x0, starting transfers between devices: 25 us -> none  [the longest x1 4.24 us: body(): lax.all_to_all(key_exp, 'uly', split_axis=1, concat_axis=0, tiled=True)]
    all_gather x2 -> x0, waiting for transfers between devices: 17.3 us -> none  [the longest x1 17.3 us: body(): lax.all_gather(value_rows, 'blk', axis=0, tiled=True)]
    reduce_sum x6 -> x0, other arithmetic: 3.64 us -> none  [the longest x4 2.82 us: attend_block(): total = total * correction + jnp.sum(weights, axis=2)]
    unnamed x29 -> x2, local copies, waits for them, and re-layouts: 5.73 us -> 2.75 us
  transfers between devices with their start and end apart: 9 -> 0, of which waited for: 5 -> 0; matrix products, arithmetic and copies ran while one was open for 33% -> 0% of each run, Pallas kernels for 0% -> 0%
where the time goes in v1:
time: 67.1 us; the launch traced here: 66 us
  Pallas kernels  60.7 us (90%)
  local copies, waits for them, and re-layouts  2.75 us (4%)
  between operations  2.58 us (4%)
    pallas_call x1, Pallas kernels, fused_body(): pl.pallas_call(functools.partial(fused_kernel, uly_size, blk_size), out_s...  60.7 us
    unnamed x2, local copies, waits for them, and re-layouts  2.75 us

profile of v1, /device:TPU:0, one launch (start us, length us, event | category | flops | bytes accessed | tf_op | source)
XLA Modules:
  0.0 66.0 jit_solution(10837852534703017855)
XLA Ops:
  2.6 60.7 %shard_map.185 = (f32[64,128]{1,0:T(8,128)}, f32[64,128]{1,0:T(8,128)}) custom-call(bf16[128,2048]{1,0:T(8,128)(2,1)} %q_hbm.1, bf16[128,2048]{1,0:T(8,128)(2,1)} %k_hbm.1, bf16[128,2048]{1,0:T(8,128)(2,1)} %v_hbm.1, bf16[256,2048]{1,0:T(8,128)(2,1)} %tk_hbm.1, bf16[256,2048]{1,0:T(8,128)(2,1)} %tv_hbm.1, s32[1]{0:T(128)S(6)} %copy.22.text_len, ...), custom_call_target="tpu_custom_call" | custom-call | tf_op jit(solution)/shard_map/pallas_call | solution.py:511
  63.3 1.4 %copy.25 = f32[128,64]{0,1:T(8,128)} copy(f32[128,64]{0,1:T(8,128)} %bitcast.13) | data formatting | bytes 65536
  64.7 1.4 %copy.26 = f32[128,64]{0,1:T(8,128)} copy(f32[128,64]{0,1:T(8,128)} %bitcast.12) | data formatting | bytes 65536

commit v2 on v1

--- a/solution.py
+++ b/solution.py
@@ -195,7 +195,8 @@
     return (velocity, next_latents)
 
 
-CHUNK = 2
+CHUNK = 4
+SUB = 2
 
 
 def block_round(entries, spread_matrix):
@@ -234,17 +235,13 @@
     fw_hbm,
     bias,
     ow_hbm,
-    uncond,
-    latents,
-    timestep,
-    guidance,
-    vel_out,
-    next_out,
+    cond_out,
     raw,
     coded,
     qbuf,
     kbuf,
     vbuf,
+    vwide,
     obuf,
     att,
     weight,
@@ -333,6 +330,16 @@
             columns = pl.ds(pl.multiple_of((u * blk_size + b) * HD, HD), HD)
             return block_round(raw[kind, :, columns], spread_matrix)
 
+        near = uly_size if kind == 2 else 1
+
+        def code_and_send_near(j, unused):
+            coded[kind, slot(j), :] = code(j)
+            outgoing(kind, target, j).start()
+            return unused
+
+        if kind == 2:
+            target[pl.ds(0, rows), :] = code(0)
+            lax.fori_loop(1, near, code_and_send_near, 0)
         if kind == 0:
 
             def code_only(i, unused):
@@ -354,8 +361,9 @@
             outgoing(kind, target, j).start()
             return unused
 
-        lax.fori_loop(first, n - 1, code_and_send, 0)
-        target[pl.ds(0, rows), :] = code(0)
+        lax.fori_loop(first, n - near, code_and_send, 0)
+        if kind != 2:
+            target[pl.ds(0, rows), :] = code(0)
 
     def start_weight(i, unused):
         weight_load(n - 1 - i).start()
@@ -370,17 +378,22 @@
 
         lax.fori_loop(0, n - 1, one, 0)
 
+    vwide[:, HD:] = jnp.ones((vwide.shape[0], HD), jnp.bfloat16)
     wait_recv(0, kbuf)
     wait_recv(1, vbuf)
     loads[3].wait()
     loads[4].wait()
+    vwide[:, :HD] = vbuf[...]
 
     factor = math.log2(math.e) / math.sqrt(HD)
-    span = CHUNK * rows
+    span = SUB * rows
     text_valid = lax.broadcasted_iota(jnp.int32, (span, text), 1) < text_len[0]
 
     def attend(first_slot):
-        q = qbuf[pl.ds(pl.multiple_of(first_slot * rows, rows), span), :]
+        start = first_slot * rows
+        if not isinstance(start, int):
+            start = pl.multiple_of(start, span)
+        q = qbuf[pl.ds(start, span), :]
         across = (((1,), (1,)), ((), ()))
         image = lax.dot_general(
             q, kbuf[pl.ds(0, n * rows), :], across, preferred_element_type=jnp.float32
@@ -394,17 +407,16 @@
         )
         image = jnp.exp2((image - peak) * factor)
         words = jnp.exp2((words - peak) * factor)
-        total = jnp.sum(image, axis=1, keepdims=True) + jnp.sum(words, axis=1, keepdims=True)
         mixed = jnp.dot(
             image.astype(jnp.bfloat16),
-            vbuf[pl.ds(0, n * rows), :],
+            vwide[pl.ds(0, n * rows), :],
             preferred_element_type=jnp.float32,
         ) + jnp.dot(
             words.astype(jnp.bfloat16),
-            vbuf[pl.ds(n * rows, text), :],
+            vwide[pl.ds(n * rows, text), :],
             preferred_element_type=jnp.float32,
         )
-        return (mixed / total).astype(jnp.bfloat16)
+        return (mixed[:, :HD] / mixed[:, HD:]).astype(jnp.bfloat16)
 
     def returning(j):
         u, b = behind(j)
@@ -417,27 +429,36 @@
             device_id_type=pl.DeviceIdType.MESH,
         )
 
+    def attend_chunk(first_slot):
+        for k in range(0, CHUNK, SUB):
+            start = (first_slot + k) * rows
+            if not isinstance(start, int):
+                start = pl.multiple_of(start, span)
+            obuf[pl.ds(start, span), :] = attend(first_slot + k)
+
     def chunk(c, unused):
         first_slot = n - CHUNK - c * CHUNK
         for k in range(CHUNK):
             outgoing(2, qbuf, first_slot + k).wait_recv()
-        obuf[pl.ds(pl.multiple_of(first_slot * rows, rows), span), :] = attend(first_slot)
+        attend_chunk(first_slot)
         for k in range(CHUNK):
             returning(first_slot + k).start()
         return unused
 
-    lax.fori_loop(0, n // CHUNK - 1, chunk, 0)
-    for k in range(1, CHUNK):
-        outgoing(2, qbuf, k).wait_recv()
-    mixed = attend(0)
-    obuf[pl.ds(0, span), :] = mixed
-    for k in range(1, CHUNK):
-        returning(k).start()
-    att[0] = mixed[:rows]
+    for first_slot in range(0, uly_size, CHUNK):
+        for k in range(first_slot, first_slot + CHUNK):
+            if k > 0:
+                outgoing(2, qbuf, k).wait_recv()
+        attend_chunk(first_slot)
+        for k in range(first_slot, first_slot + CHUNK):
+            if k > 0:
+                returning(k).start()
+    lax.fori_loop(0, (n - uly_size) // CHUNK, chunk, 0)
+    att[0] = obuf[pl.ds(0, rows), :]
 
     hidden = jnp.zeros((rows, gate.shape[1]), jnp.float32)
-    group = 4
-    for g in range(n // group - 1, -1, -1):
+    group = uly_size
+    for g in [0] + list(range(n // group - 1, 0, -1)):
         for j in range(g * group, (g + 1) * group):
             weight_load(j).wait()
             if j > 0:
@@ -460,12 +481,7 @@
     cond = lax.dot_general(
         fw[...], modulated, (((1,), (1,)), ((), ())), preferred_element_type=jnp.float32
     ) + jnp.transpose(jnp.broadcast_to(bias[...], (rows, bias.shape[1])))
-    strength = jnp.full((1, 1), guidance[0], jnp.int32).astype(jnp.float32) / 10.0
-    velocity = uncond[...] + strength * (cond - uncond[...])
-    index = jnp.full((1, 1), timestep[0], jnp.int32).astype(jnp.float32)
-    delta = sigma_of(1.0 - (index + 1.0) / STEPS) - sigma_of(1.0 - index / STEPS)
-    vel_out[...] = velocity
-    next_out[...] = latents[...] + delta * velocity
+    cond_out[...] = cond
 
     def drain(j, unused):
         outgoing(0, kbuf, j).wait_send()
@@ -508,21 +524,22 @@
     smem = pl.BlockSpec(memory_space=pltpu.SMEM)
     result = jax.ShapeDtypeStruct(latents.shape[::-1], jnp.float32)
     bf16 = jnp.bfloat16
-    velocity, next_latents = pl.pallas_call(
+    cond_velocity = pl.pallas_call(
         functools.partial(fused_kernel, uly_size, blk_size),
-        out_shape=(result, result),
+        out_shape=result,
         in_specs=[anywhere] * 5
         + [smem]
         + [anywhere] * 2
         + [vmem] * 3
-        + [anywhere, vmem, anywhere, vmem, vmem, smem, smem],
-        out_specs=(vmem, vmem),
+        + [anywhere, vmem, anywhere],
+        out_specs=vmem,
         scratch_shapes=[
             pltpu.VMEM((3, rows, HEADS * HD), bf16),
             pltpu.VMEM((3, n * rows, HD), bf16),
             pltpu.VMEM((n * rows, HD), bf16),
             pltpu.VMEM((n * rows + text, HD), bf16),
             pltpu.VMEM((n * rows + text, HD), bf16),
+            pltpu.VMEM((n * rows + text, 2 * HD), bf16),
             pltpu.VMEM((n * rows, HD), bf16),
             pltpu.VMEM((n, rows, HD), bf16),
             pltpu.VMEM((HEADS * HD, width), bf16),
@@ -554,12 +571,12 @@
         final_weight.T,
         final_bias.reshape(1, -1),
         out_weight,
-        uncond_velocity.T,
-        latents.T,
-        timestep,
-        guidance,
-    )
-    return velocity.T, next_latents.T
+    )
+    factor = guidance[0].astype(jnp.float32) / 10.0
+    velocity = uncond_velocity + factor * (cond_velocity.T - uncond_velocity)
+    index = timestep[0].astype(jnp.float32)
+    delta = sigma_of(1.0 - (index + 1.0) / STEPS) - sigma_of(1.0 - index / STEPS)
+    return velocity, latents + delta * velocity
 
 
 def solution(mesh):

time: 67.1 us -> 61.3 us (0.914); the launches traced: 66 us -> 61 us
  Pallas kernels: 60.7 us -> 56.9 us
  local copies, waits for them, and re-layouts: 2.75 us -> 0.01 us
  other arithmetic: 0 us -> 1.39 us
    pallas_call x1, Pallas kernels: 60.7 us -> 56.9 us  [fused_body(): pl.pallas_call(functools.partial(fused_kernel, uly_size, blk_size), out_s...]
    unnamed x2 -> x4, local copies, waits for them, and re-layouts: 2.75 us -> 0.01 us
    add x0 -> x1, other arithmetic: none -> 1.39 us  [fused_body(): return (velocity, latents + delta * velocity)]
where the time goes in v2:
time: 61.3 us; the launch traced here: 61 us
  Pallas kernels  56.9 us (93%)
  between operations  2.72 us (4%)
  other arithmetic  1.39 us (2%)
    pallas_call x1, Pallas kernels, fused_body(): pl.pallas_call(functools.partial(fused_kernel, uly_size, blk_size), out_s...  56.9 us
    add x1, other arithmetic, fused_body(): return (velocity, latents + delta * velocity)  1.39 us

profile of v2, /device:TPU:0, one launch (start us, length us, event | category | flops | bytes accessed | tf_op | source)
XLA Modules:
  0.0 61.0 jit_solution(8671475512872972509)
XLA Ops:
  0.6 0.0 copy-start
  0.6 0.0 copy-start.1
  2.7 56.9 %shard_map.185 = f32[64,128]{1,0:T(8,128)} custom-call(bf16[128,2048]{1,0:T(8,128)(2,1)} %q_hbm.1, bf16[128,2048]{1,0:T(8,128)(2,1)} %k_hbm.1, bf16[128,2048]{1,0:T(8,128)(2,1)} %v_hbm.1, bf16[256,2048]{1,0:T(8,128)(2,1)} %tk_hbm.1, bf16[256,2048]{1,0:T(8,128)(2,1)} %tv_hbm.1, s32[1]{0:T(128)S(6)} %copy.20.text_len, bf16[128,3072]{1,0:T(8,128)(2,1)} %res_hbm.1, ...), custom_call_target="tpu_custom_call" | custom-call | tf_op jit(solution)/shard_map/pallas_call | solution.py:527
  59.6 0.0 copy-done
  59.6 0.0 copy-done.1
  59.6 1.4 %multiply_add_fusion = (f32[128,64]{0,1:T(8,128)}, f32[128,64]{0,1:T(8,128)}) fusion(f32[128,64]{0,1:T(8,128)S(1)} %copy-done, f32[]{:T(128)} %bitcast.7, f32[128,64]{0,1:T(8,128)S(1)} %copy-done.1, f32[64,128]{1,0:T(8,128)} %shard_map.185, f32[]{:T(128)} %bitcast), kind=kLoop, calls=%fused_computation.3 | loop fusion | flops 40960 | bytes 163848 | tf_op jit(solution)/shard_map/add | solution.py:579
Async XLA Ops:
  0.6 58.9 %copy-start = (f32[128,64]{0,1:T(8,128)S(1)}, f32[128,64]{0,1:T(8,128)}, u32[]{:S(2)}) copy-start(f32[128,64]{0,1:T(8,128)} %param.33) | copy-start | bytes 98308
  0.6 58.9 %copy-start.1 = (f32[128,64]{0,1:T(8,128)S(1)}, f32[128,64]{0,1:T(8,128)}, u32[]{:S(2)}) copy-start(f32[128,64]{0,1:T(8,128)} %param.32) | copy-start | bytes 98308

commit v3 on v2

--- a/solution.py
+++ b/solution.py
@@ -226,14 +226,14 @@
     v_hbm,
     tk_hbm,
     tv_hbm,
-    text_len,
+    len_hbm,
     res_hbm,
     mlp_hbm,
-    gate,
-    shift,
-    scale,
+    gate_hbm,
+    shift_hbm,
+    scale_hbm,
     fw_hbm,
-    bias,
+    bias_hbm,
     ow_hbm,
     cond_out,
     raw,
@@ -248,6 +248,11 @@
     res,
     mlp,
     fw,
+    gate,
+    shift,
+    scale,
+    bias,
+    text_len,
     load_sem,
     weight_sem,
     send_sem,
@@ -291,6 +296,11 @@
         pltpu.make_async_copy(res_hbm, res, load_sem.at[5]),
         pltpu.make_async_copy(mlp_hbm, mlp, load_sem.at[6]),
         pltpu.make_async_copy(fw_hbm, fw, load_sem.at[7]),
+        pltpu.make_async_copy(gate_hbm, gate, load_sem.at[8]),
+        pltpu.make_async_copy(shift_hbm, shift, load_sem.at[9]),
+        pltpu.make_async_copy(scale_hbm, scale, load_sem.at[10]),
+        pltpu.make_async_copy(bias_hbm, bias, load_sem.at[11]),
+        pltpu.make_async_copy(len_hbm, text_len, load_sem.at[12]),
     ]
     for load in loads:
         load.start()
@@ -299,6 +309,9 @@
     lane_from = lax.broadcasted_iota(jnp.int32, (HD, HD), 0)
     lane_to = lax.broadcasted_iota(jnp.int32, (HD, HD), 1)
     spread_matrix = jnp.where(lane_from == lane_to // 32 * 32 + 31, 1.0, 0.0).astype(jnp.bfloat16)
+
+    def spread_slot(i):
+        return (blk_size - 1 - i % blk_size) * uly_size + uly_size - 1 - i // blk_size
 
     def slot(j):
         return pl.ds(pl.multiple_of(j * rows, rows), rows)
@@ -343,20 +356,20 @@
         if kind == 0:
 
             def code_only(i, unused):
-                j = n - 1 - i
+                j = spread_slot(i)
                 coded[kind, slot(j), :] = code(j)
                 return unused
 
             lax.fori_loop(0, 2, code_only, 0)
             pl.semaphore_wait(barrier, n - 1)
-            outgoing(kind, target, n - 1).start()
-            outgoing(kind, target, n - 2).start()
+            outgoing(kind, target, spread_slot(0)).start()
+            outgoing(kind, target, spread_slot(1)).start()
             first = 2
         else:
             first = 0
 
         def code_and_send(i, unused):
-            j = n - 1 - i
+            j = n - 1 - i if kind == 2 else spread_slot(i)
             coded[kind, slot(j), :] = code(j)
             outgoing(kind, target, j).start()
             return unused
@@ -383,6 +396,7 @@
     wait_recv(1, vbuf)
     loads[3].wait()
     loads[4].wait()
+    loads[12].wait()
     vwide[:, :HD] = vbuf[...]
 
     factor = math.log2(math.e) / math.sqrt(HD)
@@ -471,6 +485,8 @@
         )
     loads[5].wait()
     loads[6].wait()
+    for place in range(8, 12):
+        loads[place].wait()
     hidden = res[...].astype(jnp.float32) + gate[...] * (hidden + mlp[...].astype(jnp.float32))
     center = jnp.mean(hidden, axis=1, keepdims=True)
     hidden = hidden - center
@@ -521,17 +537,12 @@
     width = residual.shape[1]
     anywhere = pl.BlockSpec(memory_space=pl.ANY)
     vmem = pl.BlockSpec(memory_space=pltpu.VMEM)
-    smem = pl.BlockSpec(memory_space=pltpu.SMEM)
     result = jax.ShapeDtypeStruct(latents.shape[::-1], jnp.float32)
     bf16 = jnp.bfloat16
     cond_velocity = pl.pallas_call(
         functools.partial(fused_kernel, uly_size, blk_size),
         out_shape=result,
-        in_specs=[anywhere] * 5
-        + [smem]
-        + [anywhere] * 2
-        + [vmem] * 3
-        + [anywhere, vmem, anywhere],
+        in_specs=[anywhere] * 14,
         out_specs=vmem,
         scratch_shapes=[
             pltpu.VMEM((3, rows, HEADS * HD), bf16),
@@ -546,7 +557,12 @@
             pltpu.VMEM((rows, width), bf16),
             pltpu.VMEM((rows, width), bf16),
             pltpu.VMEM(final_weight.shape[::-1], bf16),
-            pltpu.SemaphoreType.DMA((8,)),
+            pltpu.VMEM((1, width), jnp.float32),
+            pltpu.VMEM((1, width), jnp.float32),
+            pltpu.VMEM((1, width), jnp.float32),
+            pltpu.VMEM((1, final_bias.shape[0]), jnp.float32),
+            pltpu.SMEM((1,), jnp.int32),
+            pltpu.SemaphoreType.DMA((13,)),
             pltpu.SemaphoreType.DMA((n,)),
             pltpu.SemaphoreType.DMA((3, n)),
             pltpu.SemaphoreType.DMA((3, n)),

time: 61.3 us -> 60.6 us (0.989)
  Pallas kernels: 56.9 us -> 56.2 us
    pallas_call x1, Pallas kernels: 56.9 us -> 56.2 us  [fused_body(): pl.pallas_call(functools.partial(fused_kernel, uly_size, blk_size), out_s...]
where the time goes in v3:
time: 60.6 us; the launch traced here: 60.4 us
  Pallas kernels  56.2 us (93%)
  between operations  2.72 us (4%)
  other arithmetic  1.39 us (2%)
    pallas_call x1, Pallas kernels, fused_body(): pl.pallas_call(functools.partial(fused_kernel, uly_size, blk_size), out_s...  56.2 us
    add x1, other arithmetic, fused_body(): return (velocity, latents + delta * velocity)  1.39 us

profile of v3, /device:TPU:0, one launch (start us, length us, event | category | flops | bytes accessed | tf_op | source)
XLA Modules:
  0.0 60.4 jit_solution(3144800042173386936)
XLA Ops:
  0.6 0.0 copy-start
  0.6 0.0 copy-start.1
  2.7 56.2 %shard_map.185 = f32[64,128]{1,0:T(8,128)} custom-call(bf16[128,2048]{1,0:T(8,128)(2,1)} %q_hbm.1, bf16[128,2048]{1,0:T(8,128)(2,1)} %k_hbm.1, bf16[128,2048]{1,0:T(8,128)(2,1)} %v_hbm.1, bf16[256,2048]{1,0:T(8,128)(2,1)} %tk_hbm.1, bf16[256,2048]{1,0:T(8,128)(2,1)} %tv_hbm.1, s32[1]{0:T(128)S(6)} %copy.20.len_hbm, bf16[128,3072]{1,0:T(8,128)(2,1)} %res_hbm.1, ...), custom_call_target="tpu_custom_call" | custom-call | tf_op jit(solution)/shard_map/pallas_call | solution.py:542
  58.9 0.0 copy-done
  58.9 0.0 copy-done.1
  59.0 1.4 %multiply_add_fusion = (f32[128,64]{0,1:T(8,128)}, f32[128,64]{0,1:T(8,128)}) fusion(f32[128,64]{0,1:T(8,128)S(1)} %copy-done, f32[]{:T(128)} %bitcast.7, f32[128,64]{0,1:T(8,128)S(1)} %copy-done.1, f32[64,128]{1,0:T(8,128)} %shard_map.185, f32[]{:T(128)} %bitcast), kind=kLoop, calls=%fused_computation.3 | loop fusion | flops 40960 | bytes 163848 | tf_op jit(solution)/shard_map/add | solution.py:595
Async XLA Ops:
  0.6 58.3 %copy-start = (f32[128,64]{0,1:T(8,128)S(1)}, f32[128,64]{0,1:T(8,128)}, u32[]{:S(2)}) copy-start(f32[128,64]{0,1:T(8,128)} %param.33) | copy-start | bytes 98308
  0.6 58.3 %copy-start.1 = (f32[128,64]{0,1:T(8,128)S(1)}, f32[128,64]{0,1:T(8,128)}, u32[]{:S(2)}) copy-start(f32[128,64]{0,1:T(8,128)} %param.32) | copy-start | bytes 98308
